TPU v7x, 512 devices: a whole 4x4x16 slice. The times are simulated.
512 devices in a mesh: pipe: 4 (over y), seq: 16 (over z), tensor: 8 (over x, core).
Axes of the slice: x: 4, y: 4, z: 16, core: 2. Of those that a mesh axis runs over, the one named last changes fastest.
Arguments:
- layer_input: bfloat16 [4, 2048, 8192], P('pipe', 'seq', 'tensor'), may hold values from -320 to 320
- conv_out: bfloat16 [4, 2048, 8192], P('pipe', 'seq', 'tensor'), may hold values from -8 to 8
- act_grad: bfloat16 [4, 2048, 8192], P('pipe', 'seq', 'tensor'), may hold values from -6 to 6
- conv_kernel: bfloat16 [4, 4, 8192], P('pipe', None, 'tensor'), may hold values from -3 to 3
- in_proj: bfloat16 [4, 8192, 8192], P('pipe', 'seq', 'tensor'), may hold values from -0.0625 to 0.0625
- sketch_matrix: bfloat16 [4, 8192, 512], P('pipe', 'tensor'), may hold values from -0.0625 to 0.0625
Outputs:
- passed_grad: bfloat16 [4, 2048, 8192], P('pipe', 'tensor', 'seq')
- basis: bfloat16 [4, 8192, 512], P('pipe', 'tensor')
All inputs are finite; a program needn't handle non-finite values.
Results may differ from a plain program's by a relative error of at most 0.017.
Values may be sent and summed in bfloat16 or wider, within the bound.
No kernel may reach another device: no remote copies, remote signals or barrier semaphores. Data moves between devices by JAX's collectives and lax.ppermute only.
A program may use at most 64 MiB of HBM per device.

v0:
```python
import math
import jax
import jax.numpy as jnp
from jax import lax
from jax.sharding import PartitionSpec as P

D = 8192


def passed_along(block, axis, distance):
    devices = range(lax.axis_size(axis))
    route = [(i - distance, i) for i in devices if i - distance in devices]
    return lax.ppermute(block, axis, route)


def shifted(value, axis, by):
    count = lax.axis_size(axis)
    return lax.ppermute(value, axis, [(i, (i + by) % count) for i in range(count)])


def finish_basis(sketch, gram):
    low = jnp.linalg.cholesky(gram)
    ortho_t = lax.linalg.triangular_solve(low, sketch.T, left_side=True, lower=True)
    return (ortho_t.T * math.sqrt(D)).astype(jnp.bfloat16)


def local(layer_input, conv_out, act_grad, conv_kernel, in_proj, sketch_matrix):
    acts = layer_input[0]
    kernel = conv_kernel[0]
    weights = in_proj[0]
    test_matrix = sketch_matrix[0]
    tok_rows = acts.shape[0]
    taps = kernel.shape[0]
    pval = conv_out[0].astype(jnp.float32)
    sig = jax.nn.sigmoid(pval)
    pre_grad = act_grad[0].astype(jnp.float32) * sig * (1.0 + pval * (1.0 - sig))
    ahead = passed_along(pre_grad[: taps - 1], "seq", -1)
    extended = jnp.concatenate([pre_grad, ahead], axis=0)
    total = jnp.zeros(pre_grad.shape, jnp.float32)
    for tap in range(taps):
        total = total + kernel[tap].astype(jnp.float32) * extended[tap : tap + tok_rows]
    in_grad = total.astype(jnp.bfloat16)
    partial_grad = lax.dot_general(
        lax.all_gather(in_grad, "seq", axis=0, tiled=True),
        weights,
        (((1,), (1,)), ((), ())),
        preferred_element_type=jnp.float32,
    )
    input_grad = lax.psum_scatter(
        partial_grad.astype(jnp.bfloat16), "tensor", scatter_dimension=0, tiled=True
    )
    passed = shifted(input_grad, "pipe", -1)
    row_terms = jnp.dot(in_grad, test_matrix, preferred_element_type=jnp.float32)
    sketch_rows = lax.psum(row_terms, "tensor").astype(jnp.bfloat16)
    sketch_part = lax.dot_general(
        acts, sketch_rows, (((0,), (0,)), ((), ())), preferred_element_type=jnp.float32
    )
    sketch = lax.psum(sketch_part, "seq")
    gram_part = jnp.dot(sketch.T, sketch, precision=lax.Precision.HIGHEST)
    gram = lax.psum(gram_part, "tensor")
    basis = finish_basis(sketch, gram)
    return (passed[None], basis[None])


def solution(mesh):
    placed = (
        P("pipe", "seq", "tensor"),
        P("pipe", "seq", "tensor"),
        P("pipe", "seq", "tensor"),
        P("pipe", None, "tensor"),
        P("pipe", "seq", "tensor"),
        P("pipe", "tensor", None),
    )
    return jax.shard_map(
        local,
        mesh=mesh,
        in_specs=placed,
        out_specs=(P("pipe", "tensor", "seq"), P("pipe", "tensor", None)),
        check_vma=False,
    )
```

profile of v0, /device:TPU:26, one launch (start us, length us, event | category | flops | bytes accessed | tf_op | source)
XLA Modules:
  0.0 470.1 jit_solution(17740369245081746752)
XLA Ops:
  10.8 3.5 collective-permute-done
  14.9 24.3 %all-reduce.8 = bf16[128,512]{1,0:T(8,128)(2,1)S(1)} all-reduce(f32[128,512]{1,0:T(8,128)S(1)} %fusion.15), channel_id=1, replica_groups=mesh['pipe'=4,'seq'=16,'tensor'=8] {'tensor'}, use_global_device_ids=true, to_apply=%region_1.0 | all-reduce | flops 65536 | bytes 393216 | tf_op jit(solution)/shard_map/psum | solution.py:54
  39.2 1.8 convolution_bitcast_fusion
  41.0 149.0 %all-reduce.5.cloned.1.call-done = f32[1024,512]{0,1:T(8,128)} async-done(((f32[1024,512]{0,1:T(8,128)}), f32[1024,512]{0,1:T(8,128)}) %all-reduce.5.cloned.1.call-update) | async-done | bytes 2097168 | tf_op jit(solution)/shard_map/psum | solution.py:58
  190.0 6.7 %fusion.56 = f32[512,512]{0,1:T(8,128)} fusion(f32[1024,512]{0,1:T(8,128)} %all-reduce.5.cloned.1.call-done), kind=kOutput, calls=%fused_computation.103 | convolution fusion | flops 3221225472 | bytes 3145728 | tf_op jit(solution)/shard_map/dot_general | solution.py:59
  198.0 70.5 %all-reduce.7.cloned.1.call-done = f32[512,512]{0,1:T(8,128)} async-done(((f32[512,512]{0,1:T(8,128)}), f32[512,512]{0,1:T(8,128)}) %all-reduce.7.cloned.1.call-update) | async-done | bytes 1048592 | tf_op jit(solution)/shard_map/psum | solution.py:60
  268.5 1.6 copy.9
  271.4 11.7 %cholesky.104 = f32[128,128]{1,0:T(8,128)S(1)} custom-call(f32[128,128]{1,0:T(8,128)S(1)} %cholesky.266), custom_call_target="Cholesky" | custom-call | tf_op jit(solution)/shard_map/jit(cholesky)/cholesky | solution.py:22
  283.3 9.8 %custom-call.30 = f32[1,128,128]{1,2,0:T(8,128)S(1)} custom-call(f32[1,128,128]{2,1,0:T(8,128)S(1)} %get-tuple-element.31), custom_call_target="InvertDiagBlocksLowerTriangular" | custom-call | tf_op jit(solution)/shard_map/jit(cholesky)/cholesky | solution.py:22
  295.6 11.7 %cholesky.217 = f32[128,128]{1,0:T(8,128)S(1)} custom-call(f32[128,128]{1,0:T(8,128)S(1)} %cholesky.270), custom_call_target="Cholesky" | custom-call | tf_op jit(solution)/shard_map/jit(cholesky)/cholesky | solution.py:22
  307.4 10.0 %custom-call.31 = f32[1,128,128]{1,2,0:T(8,128)S(1)} custom-call(f32[1,128,128]{2,1,0:T(8,128)S(1)} %get-tuple-element.28), custom_call_target="InvertDiagBlocksLowerTriangular" | custom-call | tf_op jit(solution)/shard_map/jit(cholesky)/cholesky | solution.py:22
  317.6 1.4 convolution_subtract_fusion.3
  319.1 11.7 %cholesky.238 = f32[128,128]{1,0:T(8,128)S(1)} custom-call(f32[128,128]{1,0:T(8,128)S(1)} %cholesky.275), custom_call_target="Cholesky" | custom-call | tf_op jit(solution)/shard_map/jit(cholesky)/cholesky | solution.py:22
  330.8 21.4 %all-gather.2.cloned.1.call-done = bf16[2048,1024]{1,0:T(8,128)(2,1)} async-done(((bf16[128,1024]{1,0:T(8,128)(2,1)}), bf16[2048,1024]{1,0:T(8,128)(2,1)}) %all-gather.2.cloned.1.call-update) | async-done | bytes 4194320 | tf_op jit(solution)/shard_map/all_gather | solution.py:44
  352.2 5.9 %convolution_convert_fusion = bf16[2048,512]{1,0:T(8,128)(2,1)} fusion(bf16[2048,1024]{1,0:T(8,128)(2,1)} %all-gather.2.cloned.1.call-done, bf16[1,512,1024]{2,1,0:T(8,128)(2,1)S(1)} %copy-done), kind=kOutput, calls=%fused_computation.2 | convolution fusion | flops 2148532224 | bytes 7340032 | tf_op jit(solution)/shard_map/dot_general | solution.py:43
  358.8 9.8 %custom-call.32 = f32[1,128,128]{1,2,0:T(8,128)S(1)} custom-call(f32[1,128,128]{2,1,0:T(8,128)S(1)} %get-tuple-element.25), custom_call_target="InvertDiagBlocksLowerTriangular" | custom-call | tf_op jit(solution)/shard_map/jit(cholesky)/cholesky | solution.py:22
  369.4 1.5 convolution_subtract_fusion.4
  370.9 11.9 %cholesky.255 = f32[128,128]{1,0:T(8,128)S(1)} custom-call(f32[128,128]{1,0:T(8,128)S(1)} %convolution_subtract_fusion.4), custom_call_target="Cholesky" | custom-call | tf_op jit(solution)/shard_map/jit(cholesky)/cholesky | solution.py:22
  388.0 2.3 select_select_fusion
  390.3 13.6 %while.1 = (s32[]{:T(128)}, f32[512,512]{1,0:T(8,128)}, s32[4,2]{0,1:T(2,128)S(1)}, f32[4,128,128]{2,1,0:T(8,128)}, s32[]{:T(128)}) while((s32[]{:T(128)}, f32[512,512]{1,0:T(8,128)}, s32[4,2]{0,1:T(2,128)S(1)}, f32[4,128,128]{2,1,0:T(8,128)}, s32[]{:T(128)}) %tuple.35), condition=%wide.while_cond, body=%wide.while_body.sunk | while | flops 2 | bytes 132205 | solution.py:23
  390.9 2.8 bitcast_dynamic-update-slice_fusion.2
  394.4 2.8 bitcast_dynamic-update-slice_fusion.2
  397.8 2.8 bitcast_dynamic-update-slice_fusion.2
  401.2 2.8 bitcast_dynamic-update-slice_fusion.2
  404.0 40.1 %custom-call.33 = f32[4,128,128]{1,2,0:T(8,128)S(1)} custom-call(f32[4,128,128]{2,1,0:T(8,128)} %get-tuple-element.9), custom_call_target="InvertDiagBlocksLowerTriangular" | custom-call | tf_op jit(solution)/shard_map/triangular_solve | solution.py:23
  444.8 1.5 convolution_subtract_fusion.1
  446.9 1.8 convolution_subtract_fusion
  450.1 2.8 fusion.7
  453.0 2.4 collective-permute-start.1
  455.4 1.7 fusion.44
  457.1 1.6 fusion.10
  460.1 2.6 collective-permute-done.1
  (69 shorter events, 20.8 us)
Async XLA Ops:
  7.2 345.0 %copy-start = (bf16[1,512,1024]{2,1,0:T(8,128)(2,1)S(1)}, bf16[1,512,1024]{2,1,0:T(8,128)(2,1)}, u32[]{:S(2)}) copy-start(bf16[1,512,1024]{2,1,0:T(8,128)(2,1)} %param.10) | copy-start | bytes 3145732
  7.2 7.4 %copy-start.9 = (bf16[1,1024,512]{2,1,0:T(8,128)(2,1)S(1)}, bf16[1,1024,512]{2,1,0:T(8,128)(2,1)}, u32[]{:S(2)}) copy-start(bf16[1,1024,512]{2,1,0:T(8,128)(2,1)} %param.11) | copy-start | bytes 3145732
  7.2 32.0 %copy-start.10 = (bf16[1,128,1024]{2,1,0:T(8,128)(2,1)S(1)}, bf16[1,128,1024]{2,1,0:T(8,128)(2,1)}, u32[]{:S(2)}) copy-start(bf16[1,128,1024]{2,1,0:T(8,128)(2,1)} %param.6) | copy-start | bytes 786436
  7.2 182.8 %all-reduce.5.cloned.1.call-start = ((), (), s32[]{:S(2)}) async-start(), calls=%async_computation.3 | async-start | bytes 4194304 | tf_op jit(solution)/shard_map/psum | solution.py:58
  8.7 5.6 %collective-permute-start = (f32[3,1024]{1,0:T(4,128)S(1)}, f32[3,1024]{1,0:T(4,128)S(1)}, u32[]{:S(2)}, u32[]{:S(2)}) collective-permute-start(f32[3,1024]{1,0:T(4,128)S(1)} %slice.150), channel_id=1, source_target_pairs={{8,0},{16,8},{24,16},{32,24},{40,32},{48,40},{56,48},{64,56},{72,6... | collective-permute-start | bytes 36872 | tf_op jit(solution)/shard_map/ppermute | solution.py:13
  14.5 26.4 %copy-start.8 = (bf16[128,1024]{1,0:T(8,128)(2,1)}, bf16[128,1024]{1,0:T(8,128)(2,1)S(1)}, u32[]{:S(2)}) copy-start(bf16[128,1024]{1,0:T(8,128)(2,1)S(1)} %fusion.22) | copy-start | bytes 786436
  41.0 227.5 %all-reduce.7.cloned.1.call-start = ((), (), s32[]{:S(2)}) async-start(), calls=%async_computation.4 | async-start | bytes 2097152 | tf_op jit(solution)/shard_map/psum | solution.py:60
  196.8 155.4 %all-gather.2.cloned.1.call-start = ((), (), s32[]{:S(2)}) async-start(), calls=%async_computation.1 | async-start | bytes 4456448 | tf_op jit(solution)/shard_map/all_gather | solution.py:44
  197.5 255.5 %reduce-scatter.2.cloned.1.call-start = ((), (), s32[]{:S(2)}) async-start(), calls=%async_computation.2 | async-start | bytes 2359296 | tf_op jit(solution)/shard_map/reduce_scatter | solution.py:49
  268.5 1.7 copy-start.6
  270.4 1.0 copy-start.7
  317.6 40.5 %copy-start.4 = (f32[512,512]{1,0:T(8,128)}, f32[512,512]{1,0:T(8,128)S(1)}, u32[]{:S(2)}) copy-start(f32[512,512]{1,0:T(8,128)S(1)} %convolution_dynamic-update-slice_fusion) | copy-start | bytes 3145732
  358.1 86.0 %copy-start.1 = (f32[1024,512]{0,1:T(8,128)S(1)}, f32[1024,512]{0,1:T(8,128)}, u32[]{:S(2)}) copy-start(f32[1024,512]{0,1:T(8,128)} %all-reduce.5.cloned.1.call-done) | copy-start | bytes 6291460
  444.8 4.6 copy-start.2
  446.9 2.4 copy-start.3
  449.3 0.8 copy-start.5
  453.0 9.7 %collective-permute-start.1 = (bf16[256,512]{1,0:T(8,128)(2,1)}, bf16[256,512]{1,0:T(8,128)(2,1)S(1)}, u32[]{:S(2)}, u32[]{:S(2)}) collective-permute-start(bf16[256,512]{1,0:T(8,128)(2,1)} %reduce-scatter.2.cloned.1.call-done), channel_id=1, source_target_pairs={{0,384},{128,0},{256,128},{384,256},{1,385},{129,1},{257,129},{385... | collective-permute-start | bytes 786440 | tf_op jit(solution)/shard_map/ppermute | solution.py:18
Sparse Core Ops, SparseCore 0:
  41.1 148.8 all-reduce.4
  196.9 71.6 all-reduce.6
  271.2 80.9 all-gather.1
  358.2 33.6 reduce-scatter.1
where the time goes:
time: 475 us; the launch traced here: 470 us
  waiting for transfers between devices  248 us (52%)
  other arithmetic  127 us (27%)
  matrix products  30.9 us (7%)
  blocking collectives  24.3 us (5%)
  local copies, waits for them, and re-layouts  19.3 us (4%)
  between operations  17 us (4%)
    psum x1, waiting for transfers between devices, local(): sketch = lax.psum(sketch_part, 'seq')  149 us
    another operation x14, other arithmetic, finish_basis(): low = jnp.linalg.cholesky(gram)  79.9 us
    psum x1, waiting for transfers between devices, local(): gram = lax.psum(gram_part, 'tensor')  70.5 us
    another operation x3, other arithmetic, finish_basis(): lax.linalg.triangular_solve(low, sketch.T, left_side=True, lower=True)  42.5 us
    psum x1, blocking collectives, local(): sketch_rows = lax.psum(row_terms, 'tensor').astype(jnp.bfloat16)  24.3 us
    all_gather x1, waiting for transfers between devices, local(): lax.all_gather(in_grad, 'seq', axis=0, tiled=True)  21.4 us
    another operation x12, local copies, waits for them, and re-layouts  13.6 us
    another operation x7, matrix products, finish_basis(): lax.linalg.triangular_solve(low, sketch.T, left_side=True, lower=True)  9.66 us
  transfers between devices with their start and end apart: 6, of which 5 were waited for; matrix products, arithmetic and copies ran while one was open for 34% of the time, Pallas kernels for 0%

commit v1 on v0

--- a/solution.py
+++ b/solution.py
@@ -57,7 +57,7 @@
     )
     sketch = lax.psum(sketch_part, "seq")
     gram_part = jnp.dot(sketch.T, sketch, precision=lax.Precision.HIGHEST)
-    gram = lax.psum(gram_part, "tensor")
+    gram = jnp.sum(lax.all_gather(gram_part, "tensor"), axis=0)
     basis = finish_basis(sketch, gram)
     return (passed[None], basis[None])
 

time: 475 us -> 518 us (1.091)
  the two profiles are of different devices: /device:TPU:26 before, /device:TPU:1 now
where the time goes in v1:
time: 518 us; the launch traced here: 511 us
  waiting for transfers between devices  280 us (54%)
  other arithmetic  131 us (25%)
  blocking collectives  30.7 us (6%)
  matrix products  29.5 us (6%)
  local copies, waits for them, and re-layouts  18.6 us (4%)
  between operations  16.9 us (3%)
  starting transfers between devices  5.3 us (1%)
    psum x1, waiting for transfers between devices, local(): sketch = lax.psum(sketch_part, 'seq')  137 us
    another operation x14, other arithmetic, finish_basis(): low = jnp.linalg.cholesky(gram)  80 us
    all_gather x1, waiting for transfers between devices, local(): gram = jnp.sum(lax.all_gather(gram_part, 'tensor'), axis=0)  53.9 us
    another operation x3, other arithmetic, finish_basis(): lax.linalg.triangular_solve(low, sketch.T, left_side=True, lower=True)  42.5 us
    all_gather x1, waiting for transfers between devices, local(): lax.all_gather(in_grad, 'seq', axis=0, tiled=True)  42 us
    reduce_scatter x1, waiting for transfers between devices, local(): lax.psum_scatter(partial_grad.astype(jnp.bfloat16), 'tensor', scatter_dim...  40.2 us
    psum x1, blocking collectives, local(): sketch_rows = lax.psum(row_terms, 'tensor').astype(jnp.bfloat16)  30.7 us
    another operation x12, local copies, waits for them, and re-layouts  14.1 us
  transfers between devices with their start and end apart: 6, of which 6 were waited for; matrix products, arithmetic and copies ran while one was open for 3% of the time, Pallas kernels for 0%

profile of v1, /device:TPU:1, one launch (start us, length us, event | category | flops | bytes accessed | tf_op | source)
XLA Modules:
  0.0 511.5 jit_solution(854500650996299584)
XLA Ops:
  7.2 1.4 fusion.30
  10.8 3.3 collective-permute-done
  16.4 30.7 %all-reduce.5 = bf16[128,512]{1,0:T(8,128)(2,1)S(1)} all-reduce(f32[128,512]{1,0:T(8,128)S(1)} %fusion.15), channel_id=1, replica_groups=mesh['pipe'=4,'seq'=16,'tensor'=8] {'tensor'}, use_global_device_ids=true, to_apply=%region_1.0 | all-reduce | flops 65536 | bytes 393216 | tf_op jit(solution)/shard_map/psum | solution.py:54
  47.2 1.8 convolution_bitcast_fusion
  49.1 42.0 %all-gather.4.cloned.1.call-done = bf16[2048,1024]{1,0:T(8,128)(2,1)} async-done(((bf16[128,1024]{1,0:T(8,128)(2,1)}), bf16[2048,1024]{1,0:T(8,128)(2,1)}) %all-gather.4.cloned.1.call-update) | async-done | bytes 4194320 | tf_op jit(solution)/shard_map/all_gather | solution.py:44
  91.0 5.9 %convolution_convert_fusion = bf16[2048,512]{1,0:T(8,128)(2,1)} fusion(bf16[2048,1024]{1,0:T(8,128)(2,1)} %all-gather.4.cloned.1.call-done, bf16[1,512,1024]{2,1,0:T(8,128)(2,1)S(1)} %copy-done), kind=kOutput, calls=%fused_computation.2 | convolution fusion | flops 2148532224 | bytes 7340032 | tf_op jit(solution)/shard_map/dot_general | solution.py:43
  97.0 137.0 %all-reduce.4.cloned.1.call-done = f32[1024,512]{0,1:T(8,128)} async-done(((f32[1024,512]{0,1:T(8,128)}), f32[1024,512]{0,1:T(8,128)}) %all-reduce.4.cloned.1.call-update) | async-done | bytes 2097168 | tf_op jit(solution)/shard_map/psum | solution.py:58
  233.9 6.8 %fusion.56 = f32[512,512]{1,0:T(8,128)} fusion(f32[1024,512]{0,1:T(8,128)} %all-reduce.4.cloned.1.call-done), kind=kOutput, calls=%fused_computation.103 | convolution fusion | flops 3221225472 | bytes 3145728 | tf_op jit(solution)/shard_map/dot_general | solution.py:59
  240.7 40.2 %reduce-scatter.2.cloned.1.call-done = bf16[256,512]{1,0:T(8,128)(2,1)} async-done(((bf16[2048,512]{1,0:T(8,128)(2,1)}), bf16[256,512]{1,0:T(8,128)(2,1)}) %reduce-scatter.2.cloned.1.call-update) | async-done | bytes 262160 | tf_op jit(solution)/shard_map/reduce_scatter | solution.py:49
  280.9 3.8 collective-permute-start.1
  284.8 3.4 collective-permute-done.1
  288.2 53.9 %all-gather.6.cloned.1.call-done = f32[4096,512]{1,0:T(8,128)} async-done(((f32[512,512]{1,0:T(8,128)}), f32[4096,512]{1,0:T(8,128)}) %all-gather.6.cloned.1.call-update) | async-done | bytes 8388624 | tf_op jit(solution)/shard_map/all_gather | solution.py:60
  342.1 4.5 reduce_sum.9
  348.2 11.7 %cholesky.104 = f32[128,128]{1,0:T(8,128)S(1)} custom-call(f32[128,128]{1,0:T(8,128)S(1)} %cholesky.266), custom_call_target="Cholesky" | custom-call | tf_op jit(solution)/shard_map/jit(cholesky)/cholesky | solution.py:22
  360.0 9.8 %custom-call.30 = f32[1,128,128]{1,2,0:T(8,128)S(1)} custom-call(f32[1,128,128]{2,1,0:T(8,128)S(1)} %get-tuple-element.33), custom_call_target="InvertDiagBlocksLowerTriangular" | custom-call | tf_op jit(solution)/shard_map/jit(cholesky)/cholesky | solution.py:22
  372.4 11.9 %cholesky.217 = f32[128,128]{1,0:T(8,128)S(1)} custom-call(f32[128,128]{1,0:T(8,128)S(1)} %cholesky.270), custom_call_target="Cholesky" | custom-call | tf_op jit(solution)/shard_map/jit(cholesky)/cholesky | solution.py:22
  384.3 9.8 %custom-call.31 = f32[1,128,128]{1,2,0:T(8,128)S(1)} custom-call(f32[1,128,128]{2,1,0:T(8,128)S(1)} %get-tuple-element.30), custom_call_target="InvertDiagBlocksLowerTriangular" | custom-call | tf_op jit(solution)/shard_map/jit(cholesky)/cholesky | solution.py:22
  396.7 11.7 %cholesky.238 = f32[128,128]{1,0:T(8,128)S(1)} custom-call(f32[128,128]{1,0:T(8,128)S(1)} %cholesky.275), custom_call_target="Cholesky" | custom-call | tf_op jit(solution)/shard_map/jit(cholesky)/cholesky | solution.py:22
  409.7 9.8 %custom-call.32 = f32[1,128,128]{1,2,0:T(8,128)S(1)} custom-call(f32[1,128,128]{2,1,0:T(8,128)S(1)} %get-tuple-element.27), custom_call_target="InvertDiagBlocksLowerTriangular" | custom-call | tf_op jit(solution)/shard_map/jit(cholesky)/cholesky | solution.py:22
  420.4 1.4 convolution_subtract_fusion.4
  421.8 11.9 %cholesky.255 = f32[128,128]{1,0:T(8,128)S(1)} custom-call(f32[128,128]{1,0:T(8,128)S(1)} %convolution_subtract_fusion.4), custom_call_target="Cholesky" | custom-call | tf_op jit(solution)/shard_map/jit(cholesky)/cholesky | solution.py:22
  438.2 2.3 select_select_fusion
  440.5 14.1 %while.1 = (s32[]{:T(128)}, f32[512,512]{1,0:T(8,128)}, s32[4,2]{0,1:T(2,128)S(1)}, f32[4,128,128]{2,1,0:T(8,128)}, s32[]{:T(128)}) while((s32[]{:T(128)}, f32[512,512]{1,0:T(8,128)}, s32[4,2]{0,1:T(2,128)S(1)}, f32[4,128,128]{2,1,0:T(8,128)}, s32[]{:T(128)}) %tuple.36), condition=%wide.while_cond, body=%wide.while_body.sunk | while | flops 2 | bytes 132705 | solution.py:23
  441.2 2.9 bitcast_dynamic-update-slice_fusion.2
  444.7 2.9 bitcast_dynamic-update-slice_fusion.2
  448.3 2.9 bitcast_dynamic-update-slice_fusion.2
  451.8 2.8 bitcast_dynamic-update-slice_fusion.2
  454.6 40.1 %custom-call.33 = f32[4,128,128]{1,2,0:T(8,128)S(1)} custom-call(f32[4,128,128]{2,1,0:T(8,128)} %get-tuple-element.9), custom_call_target="InvertDiagBlocksLowerTriangular" | custom-call | tf_op jit(solution)/shard_map/triangular_solve | solution.py:23
  495.4 1.4 convolution_subtract_fusion.1
  497.5 1.6 convolution_subtract_fusion
  499.7 2.0 fusion.7
  502.7 1.3 copy.11
  (64 shorter events, 21.7 us)
Async XLA Ops:
  7.2 83.9 %copy-start = (bf16[1,512,1024]{2,1,0:T(8,128)(2,1)S(1)}, bf16[1,512,1024]{2,1,0:T(8,128)(2,1)}, u32[]{:S(2)}) copy-start(bf16[1,512,1024]{2,1,0:T(8,128)(2,1)} %param.10) | copy-start | bytes 3145732
  7.2 8.0 %copy-start.4 = (bf16[1,1024,512]{2,1,0:T(8,128)(2,1)S(1)}, bf16[1,1024,512]{2,1,0:T(8,128)(2,1)}, u32[]{:S(2)}) copy-start(bf16[1,1024,512]{2,1,0:T(8,128)(2,1)} %param.11) | copy-start | bytes 3145732
  7.2 40.0 %copy-start.5 = (bf16[1,128,1024]{2,1,0:T(8,128)(2,1)S(1)}, bf16[1,128,1024]{2,1,0:T(8,128)(2,1)}, u32[]{:S(2)}) copy-start(bf16[1,128,1024]{2,1,0:T(8,128)(2,1)} %param.6) | copy-start | bytes 786436
  7.2 83.8 %all-gather.4.cloned.1.call-start = ((), (), s32[]{:S(2)}) async-start(), calls=%async_computation.1 | async-start | bytes 4456448 | tf_op jit(solution)/shard_map/all_gather | solution.py:44
  8.7 5.5 %collective-permute-start = (f32[3,1024]{1,0:T(4,128)S(1)}, f32[3,1024]{1,0:T(4,128)S(1)}, u32[]{:S(2)}, u32[]{:S(2)}) collective-permute-start(f32[3,1024]{1,0:T(4,128)S(1)} %slice.150), channel_id=1, source_target_pairs={{8,0},{16,8},{24,16},{32,24},{40,32},{48,40},{56,48},{64,56},{72,6... | collective-permute-start | bytes 36872 | tf_op jit(solution)/shard_map/ppermute | solution.py:13
  15.1 218.8 %all-reduce.4.cloned.1.call-start = ((), (), s32[]{:S(2)}) async-start(), calls=%async_computation.3 | async-start | bytes 4194304 | tf_op jit(solution)/shard_map/psum | solution.py:58
  49.0 231.9 %reduce-scatter.2.cloned.1.call-start = ((), (), s32[]{:S(2)}) async-start(), calls=%async_computation.2 | async-start | bytes 2359296 | tf_op jit(solution)/shard_map/reduce_scatter | solution.py:49
  96.9 245.2 %all-gather.6.cloned.1.call-start = ((), (), s32[]{:S(2)}) async-start(), calls=%async_computation.4 | async-start | bytes 9437184 | tf_op jit(solution)/shard_map/all_gather | solution.py:60
  280.9 7.3 %collective-permute-start.1 = (bf16[256,512]{1,0:T(8,128)(2,1)}, bf16[256,512]{1,0:T(8,128)(2,1)S(1)}, u32[]{:S(2)}, u32[]{:S(2)}) collective-permute-start(bf16[256,512]{1,0:T(8,128)(2,1)} %reduce-scatter.2.cloned.1.call-done), channel_id=1, source_target_pairs={{0,384},{128,0},{256,128},{384,256},{1,385},{129,1},{257,129},{385... | collective-permute-start | bytes 786440 | tf_op jit(solution)/shard_map/ppermute | solution.py:18
  288.2 53.9 %copy-start.6 = (bf16[256,512]{1,0:T(8,128)(2,1)}, bf16[256,512]{1,0:T(8,128)(2,1)S(1)}, u32[]{:S(2)}) copy-start(bf16[256,512]{1,0:T(8,128)(2,1)S(1)} %collective-permute-done.1) | copy-start | bytes 786436
  347.2 1.0 copy-start.3
  394.4 1.0 copy-start.2
  396.6 98.1 %copy-start.1 = (f32[1024,512]{0,1:T(8,128)S(1)}, f32[1024,512]{0,1:T(8,128)}, u32[]{:S(2)}) copy-start(f32[1024,512]{0,1:T(8,128)} %all-reduce.4.cloned.1.call-done) | copy-start | bytes 6291460
  502.4 1.6 copy-start.7
Sparse Core Ops, SparseCore 0:
  15.2 75.7 all-gather.3
  93.4 140.5 all-reduce.3
  236.8 44.1 reduce-scatter.1
  283.5 58.5 all-gather.5
